TPU v7x, 32 devices: a whole 2x2x4 slice. The times are simulated.
32 devices in a mesh: dp: 8 (over z, x), mp: 4 (over y, core).
Axes of the slice: x: 2, y: 2, z: 4, core: 2. Of those that a mesh axis runs over, the one named last changes fastest.
Arguments:
- layer_in: float32 [4096, 768], P(('dp', 'mp')), may hold values from -6 to 6
- node_counts: int32 [32], P('dp'), may hold values from 32 to 127, as said below
- spatial_ids: int32 [32, 128, 128], P('dp'), may hold values from 0 to 20
- path_ids: int32 [32, 5, 128, 128], P('dp'), may hold values from 0 to 1535
- ln1_gain: float32 [768], replicated, may hold values from 0.25 to 1.75
- ln1_bias: float32 [768], replicated, may hold values from -3 to 3
- w_q: bfloat16 [768, 768], P('dp', 'mp'), may hold values from -0.21875 to 0.21875
- w_k: bfloat16 [768, 768], P('dp', 'mp'), may hold values from -0.21875 to 0.21875
- w_v: bfloat16 [768, 768], P('dp', 'mp'), may hold values from -0.21875 to 0.21875
- q_bias: float32 [768], P('mp'), may hold values from -3 to 3
- v_bias: float32 [768], P('mp'), may hold values from -3 to 3
- spatial_table: bfloat16 [22, 32], replicated, may hold values from -4 to 4
- edge_table: bfloat16 [1536, 32], P('dp'), may hold values from -4 to 4
- w_o: bfloat16 [768, 768], P('dp', 'mp'), may hold values from -0.875 to 0.875
- o_bias: float32 [768], replicated, may hold values from -3 to 3
- ln2_gain: float32 [768], replicated, may hold values from 0.25 to 1.75
- ln2_bias: float32 [768], replicated, may hold values from -3 to 3
- w_in: bfloat16 [768, 768], P('dp', 'mp'), may hold values from -0.21875 to 0.21875
- in_bias: float32 [768], P('mp'), may hold values from -3 to 3
- w_out: bfloat16 [768, 768], P('dp', 'mp'), may hold values from -0.3125 to 0.3125
- out_bias: float32 [768], replicated, may hold values from -3 to 3
- cotangent: float32 [4096, 768], P(('dp', 'mp')), may hold values from -6 to 6
Outputs:
- layer_out: float32 [4096, 768], P(('dp', 'mp'))
- grad_layer_in: float32 [4096, 768], P(('dp', 'mp'))
- grad_ln1_gain: float32 [768], replicated
- grad_ln1_bias: float32 [768], replicated
- grad_w_q: float32 [768, 768], P('dp', 'mp')
- grad_w_k: float32 [768, 768], P('dp', 'mp')
- grad_w_v: float32 [768, 768], P('dp', 'mp')
- grad_q_bias: float32 [768], P('mp')
- grad_v_bias: float32 [768], P('mp')
- grad_spatial_table: float32 [22, 32], P(None, 'mp')
- grad_edge_table: float32 [1536, 32], P('dp', 'mp')
- grad_w_o: float32 [768, 768], P('dp', 'mp')
- grad_o_bias: float32 [768], replicated
- grad_ln2_gain: float32 [768], replicated
- grad_ln2_bias: float32 [768], replicated
- grad_w_in: float32 [768, 768], P('dp', 'mp')
- grad_in_bias: float32 [768], P('mp')
- grad_w_out: float32 [768, 768], P('dp', 'mp')
- grad_out_bias: float32 [768], replicated
Inputs may be any that keep to these rules, and one draw needn't show every extreme that they name: Graph g holds its virtual node in slot 0 and its nodes in slots 1 to node_counts[g]; later slots are padding. `spatial_ids`: bucket 22 - 2 stands for unreachable pairs; bucket 22 - 1 is never given.
All inputs are finite; a program needn't handle non-finite values.
Results may differ from a plain program's by a relative error of at most 0.012.
Values may be sent and summed in bfloat16 or wider, within the bound.
No kernel may reach another device: no remote copies, remote signals or barrier semaphores. Data moves between devices by JAX's collectives and lax.ppermute only.
A program may use at most 64 MiB of HBM per device.

v0:
```python
import jax
import jax.numpy as jnp
from jax import lax
from jax.sharding import PartitionSpec as P

epsilon = 1e-05
masked_score = -1e30
pair_block = 2048


def normalize(values):
    centred = values - jnp.mean(values, axis=-1, keepdims=True)
    scale = lax.rsqrt(jnp.mean(centred * centred, axis=-1, keepdims=True) + epsilon)
    return (centred * scale, scale)


def normalize_back(grad_normed, normed, scale):
    inner = grad_normed - jnp.mean(grad_normed, axis=-1, keepdims=True)
    inner = inner - normed * jnp.mean(grad_normed * normed, axis=-1, keepdims=True)
    return inner * scale


def contract_first(left, right):
    return lax.dot_general(
        left, right, (((0,), (0,)), ((), ())), preferred_element_type=jnp.float32
    )


def contract_last(left, right):
    return lax.dot_general(
        left, right, (((1,), (1,)), ((), ())), preferred_element_type=jnp.float32
    )


def bucket_flat(spatial_g, buckets):
    slots = spatial_g.shape[0]
    rows = lax.broadcasted_iota(jnp.int32, (slots, slots), 0)
    columns = lax.broadcasted_iota(jnp.int32, (slots, slots), 1)
    chosen = jnp.where((rows == 0) | (columns == 0), buckets - 1, spatial_g)
    return chosen.reshape(1, slots * slots)


def bucket_onehot(flat_ids, count, buckets):
    kinds = lax.broadcasted_iota(jnp.int32, (buckets, count), 0)
    return (flat_ids == kinds).astype(jnp.bfloat16)


def edge_counts(path_flat, start, width, edges):
    labels = lax.dynamic_slice_in_dim(path_flat, start, width, 1)
    kinds = lax.broadcasted_iota(jnp.int32, (edges, width), 0)
    total = jnp.zeros((edges, width), jnp.bfloat16)
    for hop in range(labels.shape[0]):
        total = total + (labels[hop][None, :] == kinds).astype(jnp.bfloat16)
    return total


def pair_bias(spatial_g, path_g, spatial_tab, edge_tab, start, count):
    slots = spatial_g.shape[0]
    pairs = slots * slots
    flat_ids = bucket_flat(spatial_g, spatial_tab.shape[0])
    bias = contract_first(spatial_tab, bucket_onehot(flat_ids, count, spatial_tab.shape[0]))
    path_flat = path_g.reshape(path_g.shape[0], pairs)
    width = min(count, pair_block)

    def block_terms(offset):
        return contract_first(
            edge_tab, edge_counts(path_flat, start + offset, width, edge_tab.shape[0])
        )

    terms = lax.map(block_terms, jnp.arange(count // width, dtype=jnp.int32) * width)
    terms = jnp.transpose(terms, (1, 0, 2)).reshape(bias.shape)
    return bias + terms / path_g.shape[0]


def graph_scores(query, keys, bias, count):
    slots, heads, depth = query.shape
    scores = jnp.einsum(
        "qhd,khd->hqk", query, keys, preferred_element_type=jnp.float32
    ) * depth ** (-0.5)
    scores = scores + bias.reshape(heads, slots, slots)
    places = lax.broadcasted_iota(jnp.int32, (1, 1, slots), 2)
    return jnp.where(places <= count, scores, masked_score)


def attend_graph(query, keys, values, bias, count):
    scores = graph_scores(query, keys, bias, count)
    top = jnp.max(scores, axis=-1, keepdims=True)
    weights = jnp.exp(scores - top)
    total = jnp.sum(weights, axis=-1, keepdims=True)
    probs = (weights / total).astype(jnp.bfloat16)
    attended = jnp.einsum("hqk,khd->qhd", probs, values, preferred_element_type=jnp.float32)
    return (attended.astype(jnp.bfloat16), top + jnp.log(total))


def attend_graph_back(query, keys, values, bias, count, log_total, grad_attended):
    depth = query.shape[-1]
    scores = graph_scores(query, keys, bias, count)
    probs = jnp.exp(scores - log_total)
    grad_probs = jnp.einsum(
        "qhd,khd->hqk", grad_attended, values, preferred_element_type=jnp.float32
    )
    grad_values = jnp.einsum(
        "hqk,qhd->khd",
        probs.astype(jnp.bfloat16),
        grad_attended,
        preferred_element_type=jnp.float32,
    )
    grad_scores = probs * (grad_probs - jnp.sum(probs * grad_probs, axis=-1, keepdims=True))
    grad_scores = grad_scores.astype(jnp.bfloat16)
    grad_query = jnp.einsum(
        "hqk,khd->qhd", grad_scores, keys, preferred_element_type=jnp.float32
    ) * depth ** (-0.5)
    grad_keys = jnp.einsum(
        "hqk,qhd->khd", grad_scores, query, preferred_element_type=jnp.float32
    ) * depth ** (-0.5)
    return (
        grad_query.astype(jnp.bfloat16),
        grad_keys.astype(jnp.bfloat16),
        grad_values.astype(jnp.bfloat16),
        grad_scores,
    )


def table_grads(spatial_g, path_g, piece, start, spatial_grad, edge_grad):
    count = piece.shape[1]
    pairs = spatial_g.shape[0] * spatial_g.shape[1]
    flat_ids = bucket_flat(spatial_g, spatial_grad.shape[0])
    spatial_grad = spatial_grad + contract_last(
        bucket_onehot(flat_ids, count, spatial_grad.shape[0]), piece
    )
    path_flat = path_g.reshape(path_g.shape[0], pairs)
    width = min(count, pair_block)

    def add_block(index, total):
        offset = index * width
        counts = edge_counts(path_flat, start + offset, width, edge_grad.shape[0])
        block = lax.dynamic_slice_in_dim(piece, offset, width, 1)
        return total + contract_last(counts, block)

    edge_grad = lax.fori_loop(0, count // width, add_block, edge_grad)
    return (spatial_grad, edge_grad)


def local(
    layer_in,
    node_counts,
    spatial_ids,
    path_ids,
    ln1_gain,
    ln1_bias,
    w_q,
    w_k,
    w_v,
    q_bias,
    v_bias,
    spatial_table,
    edge_table,
    w_o,
    o_bias,
    ln2_gain,
    ln2_bias,
    w_in,
    in_bias,
    w_out,
    out_bias,
    cotangent,
):
    graphs, slots = (spatial_ids.shape[0], spatial_ids.shape[1])
    pairs = slots * slots
    all_heads = spatial_table.shape[1]
    heads = all_heads // lax.axis_size("mp")
    head_width = w_q.shape[1]
    ff_width = w_in.shape[1]
    depth = head_width // heads
    split_shape = (graphs, slots, heads, depth)
    row_count = graphs * slots
    head_start = lax.axis_index("mp") * heads
    gathered = (
        lax.all_gather(w_q, "dp", axis=0, tiled=True),
        lax.all_gather(w_k, "dp", axis=0, tiled=True),
        lax.all_gather(w_v, "dp", axis=0, tiled=True),
        lax.all_gather(w_o, "dp", axis=0, tiled=True),
        lax.all_gather(w_in, "dp", axis=0, tiled=True),
        lax.all_gather(w_out, "dp", axis=0, tiled=True),
        lax.all_gather(edge_table, "dp", axis=0, tiled=True),
    )
    full_q, full_k, full_v, full_o, full_in, full_out, full_edge = gathered
    first_normed, first_scale = normalize(layer_in)
    h1 = lax.all_gather(
        (first_normed * ln1_gain + ln1_bias).astype(jnp.bfloat16), "mp", axis=0, tiled=True
    )
    query = (jnp.dot(h1, full_q, preferred_element_type=jnp.float32) + q_bias).astype(jnp.bfloat16)
    keys = jnp.dot(h1, full_k, preferred_element_type=jnp.float32).astype(jnp.bfloat16)
    values = (jnp.dot(h1, full_v, preferred_element_type=jnp.float32) + v_bias).astype(jnp.bfloat16)
    query_split = query.reshape(split_shape)
    keys_split = keys.reshape(split_shape)
    values_split = values.reshape(split_shape)
    local_spatial = lax.dynamic_slice_in_dim(spatial_table, head_start, heads, 1)
    local_edge = lax.dynamic_slice_in_dim(full_edge, head_start, heads, 1)

    def head_bias(item):
        return pair_bias(item[0], item[1], local_spatial, local_edge, 0, pairs)

    biases = lax.map(head_bias, (spatial_ids, path_ids))

    def forward_graph(item):
        query_g, keys_g, values_g, bias, count = item
        return attend_graph(query_g, keys_g, values_g, bias, count)

    attended, log_total = lax.map(
        forward_graph, (query_split, keys_split, values_split, biases, node_counts)
    )
    attended = attended.reshape(row_count, head_width)
    branch = lax.psum_scatter(
        contract_last(attended, full_o), "mp", scatter_dimension=0, tiled=True
    )
    mid = layer_in + branch + o_bias
    second_normed, second_scale = normalize(mid)
    h2 = lax.all_gather(
        (second_normed * ln2_gain + ln2_bias).astype(jnp.bfloat16), "mp", axis=0, tiled=True
    )
    pre = jnp.dot(h2, full_in, preferred_element_type=jnp.float32) + in_bias
    hidden = jax.nn.gelu(pre, approximate=False).astype(jnp.bfloat16)
    feed = lax.psum_scatter(
        contract_last(hidden, full_out).astype(jnp.bfloat16), "mp", scatter_dimension=0, tiled=True
    ).astype(jnp.float32)
    layer_out = mid + feed + out_bias
    grad_ffn = lax.all_gather(cotangent.astype(jnp.bfloat16), "mp", axis=0, tiled=True)
    grad_w_out = contract_first(grad_ffn, hidden)
    grad_hidden = jnp.dot(grad_ffn, full_out, preferred_element_type=jnp.float32)
    unused, gelu_back = jax.vjp(lambda inner: jax.nn.gelu(inner, approximate=False), pre)
    grad_pre = gelu_back(grad_hidden)[0].astype(jnp.bfloat16)
    grad_w_in = contract_first(h2, grad_pre)
    grad_h2 = lax.psum_scatter(
        contract_last(grad_pre, full_in), "mp", scatter_dimension=0, tiled=True
    )
    grad_mid = cotangent + normalize_back(grad_h2 * ln2_gain, second_normed, second_scale)
    grad_branch = lax.all_gather(grad_mid.astype(jnp.bfloat16), "mp", axis=0, tiled=True)
    grad_w_o = contract_first(grad_branch, attended)
    grad_attended = jnp.dot(grad_branch, full_o, preferred_element_type=jnp.float32).astype(
        jnp.bfloat16
    )

    def backward_graph(item):
        query_g, keys_g, values_g, bias, count, log_g, grad_g = item
        return attend_graph_back(query_g, keys_g, values_g, bias, count, log_g, grad_g)

    grad_query, grad_keys, grad_values, grad_scores = lax.map(
        backward_graph,
        (
            query_split,
            keys_split,
            values_split,
            biases,
            node_counts,
            log_total,
            grad_attended.reshape(split_shape),
        ),
    )
    score_rows = grad_scores.reshape(graphs, heads, pairs)

    def table_step(carry, item):
        spatial_g, path_g, piece = item
        return (table_grads(spatial_g, path_g, piece, table_start, carry[0], carry[1]), 0)

    table_start = 0
    start_grads = (
        jnp.zeros((spatial_table.shape[0], heads), jnp.float32),
        jnp.zeros((full_edge.shape[0], heads), jnp.float32),
    )
    table_sums, unused_steps = lax.scan(
        table_step, start_grads, (spatial_ids, path_ids, score_rows)
    )
    spatial_full = lax.dynamic_update_slice_in_dim(
        jnp.zeros((spatial_table.shape[0], all_heads), jnp.float32), table_sums[0], head_start, 1
    )
    grad_edge = table_sums[1]
    grad_edge = grad_edge / path_ids.shape[1]
    grad_query = grad_query.reshape(row_count, head_width)
    grad_keys = grad_keys.reshape(row_count, head_width)
    grad_values = grad_values.reshape(row_count, head_width)
    grad_w_q = contract_first(h1, grad_query)
    grad_w_k = contract_first(h1, grad_keys)
    grad_w_v = contract_first(h1, grad_values)
    input_terms = contract_last(grad_query, full_q) + contract_last(grad_keys, full_k)
    input_terms = input_terms + contract_last(grad_values, full_v)
    grad_h1 = lax.psum_scatter(input_terms, "mp", scatter_dimension=0, tiled=True)
    grad_layer_in = grad_mid + normalize_back(grad_h1 * ln1_gain, first_normed, first_scale)
    summed = (
        lax.psum_scatter(grad_w_q, "dp", scatter_dimension=0, tiled=True),
        lax.psum_scatter(grad_w_k, "dp", scatter_dimension=0, tiled=True),
        lax.psum_scatter(grad_w_v, "dp", scatter_dimension=0, tiled=True),
        lax.psum_scatter(grad_w_o, "dp", scatter_dimension=0, tiled=True),
        lax.psum_scatter(grad_w_in, "dp", scatter_dimension=0, tiled=True),
        lax.psum_scatter(grad_w_out, "dp", scatter_dimension=0, tiled=True),
        lax.psum_scatter(grad_edge, "dp", scatter_dimension=0, tiled=True),
    )
    model_width = layer_in.shape[1]
    feature_start = lax.axis_index("mp") * head_width
    hidden_start = lax.axis_index("mp") * ff_width
    query_full = lax.dynamic_update_slice_in_dim(
        jnp.zeros((model_width,), jnp.float32),
        jnp.sum(grad_query.astype(jnp.float32), axis=0),
        feature_start,
        0,
    )
    value_full = lax.dynamic_update_slice_in_dim(
        jnp.zeros((model_width,), jnp.float32),
        jnp.sum(grad_values.astype(jnp.float32), axis=0),
        feature_start,
        0,
    )
    hidden_full = lax.dynamic_update_slice_in_dim(
        jnp.zeros((ff_width * lax.axis_size("mp"),), jnp.float32),
        jnp.sum(grad_pre.astype(jnp.float32), axis=0),
        hidden_start,
        0,
    )
    norm_totals = lax.psum(
        (
            jnp.sum(grad_h1 * first_normed, axis=0),
            jnp.sum(grad_h1, axis=0),
            jnp.sum(grad_h2 * second_normed, axis=0),
            jnp.sum(grad_h2, axis=0),
            jnp.sum(grad_mid, axis=0),
            jnp.sum(cotangent, axis=0),
            query_full,
            value_full,
            hidden_full,
            spatial_full,
        ),
        ("dp", "mp"),
    )
    grad_q_bias = lax.dynamic_slice_in_dim(norm_totals[6], feature_start, head_width, 0)
    grad_v_bias = lax.dynamic_slice_in_dim(norm_totals[7], feature_start, head_width, 0)
    grad_in_bias = lax.dynamic_slice_in_dim(norm_totals[8], hidden_start, ff_width, 0)
    grad_spatial = lax.dynamic_slice_in_dim(norm_totals[9], head_start, heads, 1)
    return (
        layer_out,
        grad_layer_in,
        norm_totals[0],
        norm_totals[1],
        summed[0],
        summed[1],
        summed[2],
        grad_q_bias,
        grad_v_bias,
        grad_spatial,
        summed[6],
        summed[3],
        norm_totals[4],
        norm_totals[2],
        norm_totals[3],
        summed[4],
        grad_in_bias,
        summed[5],
        norm_totals[5],
    )


def solution(mesh):
    return jax.shard_map(
        local,
        mesh=mesh,
        in_specs=(
            P(("dp", "mp"), None),
            P("dp"),
            P("dp", None, None),
            P("dp", None, None, None),
            P(),
            P(),
            P("dp", "mp"),
            P("dp", "mp"),
            P("dp", "mp"),
            P("mp"),
            P("mp"),
            P(),
            P("dp", None),
            P("dp", "mp"),
            P(),
            P(),
            P(),
            P("dp", "mp"),
            P("mp"),
            P("dp", "mp"),
            P(),
            P(("dp", "mp"), None),
        ),
        out_specs=(
            P(("dp", "mp"), None),
            P(("dp", "mp"), None),
            P(),
            P(),
            P("dp", "mp"),
            P("dp", "mp"),
            P("dp", "mp"),
            P("mp"),
            P("mp"),
            P(None, "mp"),
            P("dp", "mp"),
            P("dp", "mp"),
            P(),
            P(),
            P(),
            P("dp", "mp"),
            P("mp"),
            P("dp", "mp"),
            P(),
        ),
        check_vma=False,
    )
```

profile of v0, /device:TPU:0, one launch (start us, length us, event | category | flops | bytes accessed | tf_op | source)
XLA Modules:
  0.0 1440.9 jit_solution(12586913065994715846)
XLA Ops:
  7.3 32.5 %all-gather = bf16[8,192,32]{1,2,0:T(8,128)(2,1)S(1)} all-gather(bf16[1,192,32]{1,2,0:T(8,128)(2,1)} %bitcast.346), channel_id=1, replica_groups=mesh['dp'=8,'mp'=4] {'dp'}, dimensions={0}, use_global_device_ids=true | all-gather | bytes 110592 | tf_op jit(solution)/shard_map/all_gather | solution.py:185
  40.2 307.6 %while.76 = (s32[]{:T(128)}, f32[4,8,16384]{2,1,0:T(8,128)}, s32[4,128,128]{2,1,0:T(8,128)}, bf16[22,8]{0,1:T(8,128)(2,1)S(1)}, s32[4,5,128,128]{3,2,1,0:T(8,128...) while((s32[]{:T(128)}, f32[4,8,16384]{2,1,0:T(8,128)}, ...), condition=%wide.region_5.6_spmd, body=%wide.region_2.5_spmd.sunk | while | flops 119668880 | bytes 3820008 | solution.py:204
  41.5 73.4 %while.81 = (s32[]{:T(128)}, f32[8,8,2048]{2,1,0:T(8,128)S(1)}, s32[8]{0:T(128)S(1)}, s32[5,16384]{1,0:T(8,128)S(1)}, bf16[1536,8]{0,1:T(8,128)(2,1)S(1)}, /*ind...) while((s32[]{:T(128)}, f32[8,8,2048]{2,1,0:T(8,128)S(1)}, s32[8]{0:T(128)S(1)}, ...), condition=%wide.region_4.4_spmd, body=%wide.region_3.3_spmd.sunk | while | flops 113246216 | bytes 213227 | solution.py:70
  118.4 73.4 %while.81 = (s32[]{:T(128)}, f32[8,8,2048]{2,1,0:T(8,128)S(1)}, s32[8]{0:T(128)S(1)}, s32[5,16384]{1,0:T(8,128)S(1)}, bf16[1536,8]{0,1:T(8,128)(2,1)S(1)}, /*ind...) while((s32[]{:T(128)}, f32[8,8,2048]{2,1,0:T(8,128)S(1)}, s32[8]{0:T(128)S(1)}, ...), condition=%wide.region_4.4_spmd, body=%wide.region_3.3_spmd.sunk | while | flops 113246216 | bytes 213227 | solution.py:70
  195.3 73.4 %while.81 = (s32[]{:T(128)}, f32[8,8,2048]{2,1,0:T(8,128)S(1)}, s32[8]{0:T(128)S(1)}, s32[5,16384]{1,0:T(8,128)S(1)}, bf16[1536,8]{0,1:T(8,128)(2,1)S(1)}, /*ind...) while((s32[]{:T(128)}, f32[8,8,2048]{2,1,0:T(8,128)S(1)}, s32[8]{0:T(128)S(1)}, ...), condition=%wide.region_4.4_spmd, body=%wide.region_3.3_spmd.sunk | while | flops 113246216 | bytes 213227 | solution.py:70
  272.2 73.4 %while.81 = (s32[]{:T(128)}, f32[8,8,2048]{2,1,0:T(8,128)S(1)}, s32[8]{0:T(128)S(1)}, s32[5,16384]{1,0:T(8,128)S(1)}, bf16[1536,8]{0,1:T(8,128)(2,1)S(1)}, /*ind...) while((s32[]{:T(128)}, f32[8,8,2048]{2,1,0:T(8,128)S(1)}, s32[8]{0:T(128)S(1)}, ...), condition=%wide.region_4.4_spmd, body=%wide.region_3.3_spmd.sunk | while | flops 113246216 | bytes 213227 | solution.py:70
  348.7 8.7 all_gather.33
  357.4 31.2 %all_gather.34 = bf16[768,192]{1,0:T(8,128)(2,1)S(1)} all-gather(bf16[96,192]{1,0:T(8,128)(2,1)S(1)} %copy-done.34), channel_id=1, replica_groups=mesh['dp'=8,'mp'=4] {'dp'}, dimensions={0}, use_global_device_ids=true | all-gather | bytes 331776 | tf_op jit(solution)/shard_map/all_gather | solution.py:181
  389.9 31.0 %all_gather.35 = bf16[768,192]{1,0:T(8,128)(2,1)S(1)} all-gather(bf16[96,192]{1,0:T(8,128)(2,1)S(1)} %copy-done.35), channel_id=1, replica_groups=mesh['dp'=8,'mp'=4] {'dp'}, dimensions={0}, use_global_device_ids=true | all-gather | bytes 331776 | tf_op jit(solution)/shard_map/all_gather | solution.py:179
  421.4 31.1 %all_gather.36 = bf16[768,192]{1,0:T(8,128)(2,1)S(1)} all-gather(bf16[96,192]{1,0:T(8,128)(2,1)S(1)} %copy-done.36), channel_id=1, replica_groups=mesh['dp'=8,'mp'=4] {'dp'}, dimensions={0}, use_global_device_ids=true | all-gather | bytes 331776 | tf_op jit(solution)/shard_map/all_gather | solution.py:180
  453.1 15.5 %while.77 = (s32[]{:T(128)}, bf16[4,128,8,24]{1,3,2,0:T(8,128)(2,1)S(1)}, f32[4,8,128,1]{2,1,3,0:T(8,128)}, bf16[4,128,8,24]{1,3,2,0:T(8,128)(2,1)S(1)}, s32[4]{...) while((s32[]{:T(128)}, ...), condition=%wide.region_9.10_spmd, body=%wide.region_6.9_spmd.sunk | while | flops 13786242 | bytes 5475569 | solution.py:210
  468.8 31.5 %all_gather.38 = bf16[768,192]{1,0:T(8,128)(2,1)S(1)} all-gather(bf16[96,192]{1,0:T(8,128)(2,1)S(1)} %copy-done.37), channel_id=1, replica_groups=mesh['dp'=8,'mp'=4] {'dp'}, dimensions={0}, use_global_device_ids=true | all-gather | bytes 331776 | tf_op jit(solution)/shard_map/all_gather | solution.py:182
  502.0 31.3 %all_gather.40 = bf16[768,192]{1,0:T(8,128)(2,1)S(1)} all-gather(bf16[96,192]{1,0:T(8,128)(2,1)S(1)} %copy-done.38), channel_id=1, replica_groups=mesh['dp'=8,'mp'=4] {'dp'}, dimensions={0}, use_global_device_ids=true | all-gather | bytes 331776 | tf_op jit(solution)/shard_map/all_gather | solution.py:183
  533.2 31.2 %all_gather.41 = bf16[768,192]{1,0:T(8,128)(2,1)S(1)} all-gather(bf16[96,192]{1,0:T(8,128)(2,1)} %param.53), channel_id=1, replica_groups=mesh['dp'=8,'mp'=4] {'dp'}, dimensions={0}, use_global_device_ids=true | all-gather | bytes 331776 | tf_op jit(solution)/shard_map/all_gather | solution.py:184
  575.1 8.9 all_gather.39
  592.7 26.6 %reduce-scatter.20.cloned.1.call-done = f32[128,768]{1,0:T(8,128)} async-done(((f32[512,768]{1,0:T(8,128)}), f32[128,768]{1,0:T(8,128)}) %reduce-scatter.20.cloned.1.call-update) | async-done | bytes 393232 | tf_op jit(solution)/shard_map/reduce_scatter | solution.py:234
  621.1 24.0 %reduce-scatter.18.cloned.1.call-done = bf16[128,768]{1,0:T(8,128)(2,1)} async-done(((bf16[512,768]{1,0:T(8,128)(2,1)}), bf16[128,768]{1,0:T(8,128)(2,1)}) %reduce-scatter.18.cloned.1.call-update) | async-done | bytes 196624 | tf_op jit(solution)/shard_map/reduce_scatter | solution.py:224
  657.7 26.1 %while.78 = (s32[]{:T(128)}, bf16[4,128,8,24]{1,3,2,0:T(8,128)(2,1)S(1)}, bf16[4,128,8,24]{1,3,2,0:T(8,128)(2,1)S(1)}, bf16[4,128,8,24]{1,3,2,0:T(8,128)(2,1)S(1...) while((s32[]{:T(128)}, ...), condition=%wide.region_19.20_spmd, body=%wide.region_17.19_spmd.sunk | while | flops 32889984 | bytes 9169173 | solution.py:248
  688.2 258.5 %while.80 = (s32[]{:T(128)}, f32[22,8]{0,1:T(8,128)S(1)}, f32[1536,8]{0,1:T(8,128)S(1)}, s32[4,128,128]{2,1,0:T(8,128)}, bf16[4,8,16384]{2,1,0:T(8,128)(2,1)}, /...) while((s32[]{:T(128)}, f32[22,8]{0,1:T(8,128)S(1)}, ...), condition=%wide.region_37.38_spmd.clone, body=%wide.region_34.37_spmd.clone.sunk | while | flops 119419368 | bytes 2550782 | solution.py:271
  691.8 61.1 %while.82 = (s32[]{:T(128)}, f32[1536,8]{0,1:T(8,128)S(1)}, s32[5,16384]{1,0:T(8,128)S(1)}, bf16[8,16384]{1,0:T(8,128)(2,1)S(1)}, s32[]{:T(128)}, /*index=5*/s32...) while((s32[]{:T(128)}, f32[1536,8]{0,1:T(8,128)S(1)}, s32[5,16384]{1,0:T(8,128)S(1)}, ...), condition=%wide.region_36.36_spmd, body=%wide.region_35.35_spmd.sunk | while | flops 113258504 | bytes 254187 | solution.py:140
  756.4 61.1 %while.82 = (s32[]{:T(128)}, f32[1536,8]{0,1:T(8,128)S(1)}, s32[5,16384]{1,0:T(8,128)S(1)}, bf16[8,16384]{1,0:T(8,128)(2,1)S(1)}, s32[]{:T(128)}, /*index=5*/s32...) while((s32[]{:T(128)}, f32[1536,8]{0,1:T(8,128)S(1)}, s32[5,16384]{1,0:T(8,128)S(1)}, ...), condition=%wide.region_36.36_spmd, body=%wide.region_35.35_spmd.sunk | while | flops 113258504 | bytes 254187 | solution.py:140
  821.0 61.1 %while.82 = (s32[]{:T(128)}, f32[1536,8]{0,1:T(8,128)S(1)}, s32[5,16384]{1,0:T(8,128)S(1)}, bf16[8,16384]{1,0:T(8,128)(2,1)S(1)}, s32[]{:T(128)}, /*index=5*/s32...) while((s32[]{:T(128)}, f32[1536,8]{0,1:T(8,128)S(1)}, s32[5,16384]{1,0:T(8,128)S(1)}, ...), condition=%wide.region_36.36_spmd, body=%wide.region_35.35_spmd.sunk | while | flops 113258504 | bytes 254187 | solution.py:140
  885.6 61.1 %while.82 = (s32[]{:T(128)}, f32[1536,8]{0,1:T(8,128)S(1)}, s32[5,16384]{1,0:T(8,128)S(1)}, bf16[8,16384]{1,0:T(8,128)(2,1)S(1)}, s32[]{:T(128)}, /*index=5*/s32...) while((s32[]{:T(128)}, f32[1536,8]{0,1:T(8,128)S(1)}, s32[5,16384]{1,0:T(8,128)S(1)}, ...), condition=%wide.region_36.36_spmd, body=%wide.region_35.35_spmd.sunk | while | flops 113258504 | bytes 254187 | solution.py:140
  962.5 48.5 %reduce-scatter.34.cloned.1.call-done = f32[192,8]{1,0:T(8,128)} async-done(((f32[1536,8]{1,0:T(8,128)}), f32[192,8]{1,0:T(8,128)}) %reduce-scatter.34.cloned.1.call-update) | async-done | bytes 6160
  1012.5 28.0 %reduce-scatter.22.cloned.1.call-done = f32[128,768]{1,0:T(8,128)} async-done(((f32[512,768]{1,0:T(8,128)}), f32[128,768]{1,0:T(8,128)}) %reduce-scatter.22.cloned.1.call-update) | async-done | bytes 393232 | tf_op jit(solution)/shard_map/reduce_scatter | solution.py:287
  1041.8 40.8 %all-reduce = (f32[768]{0:T(1024)}, f32[768]{0:T(1024)}, f32[768]{0:T(1024)S(1)}, f32[768]{0:T(1024)S(1)}, f32[22,32]{0,1:T(8,128)S(1)}, /*index=5*/f32[768]{0:T...) all-reduce(f32[768]{0:T(1024)S(1)} %get-tuple-element.487, ...), channel_id=1, replica_groups=mesh['dp'=8,'mp'=4] {'dp','mp'}, use_global_device_ids=true, to_apply=%region_24.25 | all-reduce | flops 7616 | bytes 60928 | tf_op jit(solution)/shard_map/psum | solution.py:319
  1087.0 20.0 %reduce-scatter.32.cloned.1.call-done = f32[96,192]{1,0:T(8,128)} async-done(((f32[768,192]{1,0:T(8,128)}), f32[96,192]{1,0:T(8,128)}) %reduce-scatter.32.cloned.1.call-update) | async-done | bytes 73744 | tf_op jit(solution)/shard_map/reduce_scatter | solution.py:294
  1107.1 65.4 %reduce-scatter.36.cloned.1.call-done = f32[96,192]{1,0:T(8,128)} async-done(((f32[768,192]{1,0:T(8,128)}), f32[96,192]{1,0:T(8,128)}) %reduce-scatter.36.cloned.1.call-update) | async-done | bytes 73744
  1172.4 65.7 %reduce-scatter.30.cloned.1.call-done = f32[96,192]{1,0:T(8,128)} async-done(((f32[768,192]{1,0:T(8,128)}), f32[96,192]{1,0:T(8,128)}) %reduce-scatter.30.cloned.1.call-update) | async-done | bytes 73744 | tf_op jit(solution)/shard_map/reduce_scatter | solution.py:293
  1238.1 65.3 %reduce-scatter.24.cloned.1.call-done = f32[96,192]{1,0:T(8,128)} async-done(((f32[768,192]{1,0:T(8,128)}), f32[96,192]{1,0:T(8,128)}) %reduce-scatter.24.cloned.1.call-update) | async-done | bytes 73744 | tf_op jit(solution)/shard_map/reduce_scatter | solution.py:290
  1303.4 65.5 %reduce-scatter.26.cloned.1.call-done = f32[96,192]{1,0:T(8,128)} async-done(((f32[768,192]{1,0:T(8,128)}), f32[96,192]{1,0:T(8,128)}) %reduce-scatter.26.cloned.1.call-update) | async-done | bytes 73744 | tf_op jit(solution)/shard_map/reduce_scatter | solution.py:291
  1368.9 65.4 %reduce-scatter.28.cloned.1.call-done = f32[96,192]{1,0:T(8,128)} async-done(((f32[768,192]{1,0:T(8,128)}), f32[96,192]{1,0:T(8,128)}) %reduce-scatter.28.cloned.1.call-update) | async-done | bytes 73744 | tf_op jit(solution)/shard_map/reduce_scatter | solution.py:292
  (539 shorter events, 610.1 us)
Async XLA Ops:
  7.2 565.6 %reduce-scatter.16.cloned.1.call-start = ((), (), s32[]{:S(2)}) async-start(), calls=%async_computation.11 | async-start | bytes 1966080 | tf_op jit(solution)/shard_map/reduce_scatter | solution.py:214
  40.2 307.6 %copy-start.3 = (f32[128,768]{1,0:T(8,128)S(1)}, f32[128,768]{1,0:T(8,128)}, u32[]{:S(2)}) copy-start(f32[128,768]{1,0:T(8,128)} %param.34) | copy-start | bytes 1179652
  40.2 307.9 %copy-start.40 = (f32[768]{0:T(1024)S(1)}, f32[768]{0:T(1024)}, u32[]{:S(2)}) copy-start(f32[768]{0:T(1024)} %param.38) | copy-start | bytes 9220
  40.2 307.9 %copy-start.52 = (f32[768]{0:T(1024)S(1)}, f32[768]{0:T(1024)}, u32[]{:S(2)}) copy-start(f32[768]{0:T(1024)} %param.39) | copy-start | bytes 9220
  348.7 72.2 %copy-start.57 = (f32[192]{0:T(256)S(1)}, f32[192]{0:T(256)}, u32[]{:S(2)}) copy-start(f32[192]{0:T(256)} %param.43) | copy-start | bytes 2308
  357.4 95.1 %copy-start.1 = (bf16[512,768]{1,0:T(8,128)(2,1)}, bf16[512,768]{1,0:T(8,128)(2,1)S(1)}, u32[]{:S(2)}) copy-start(bf16[512,768]{1,0:T(8,128)(2,1)S(1)} %all_gather.33) | copy-start | bytes 2359300
  468.8 64.4 %copy-start.16 = (bf16[4,128,8,24]{1,0,3,2:T(4,128)(2,1)}, bf16[4,128,8,24]{1,0,3,2:T(4,128)(2,1)S(1)}, u32[]{:S(2)}) copy-start(bf16[4,128,8,24]{1,0,3,2:T(4,128)(2,1)S(1)} %copy.108) | copy-start | bytes 589828
  500.3 64.1 %copy-start.29 = (f32[128,768]{1,0:T(8,128)S(1)}, f32[128,768]{1,0:T(8,128)}, u32[]{:S(2)}) copy-start(f32[128,768]{1,0:T(8,128)} %param.55) | copy-start | bytes 1179652
  501.9 71.0 %copy-start.53 = (f32[768]{0:T(1024)S(1)}, f32[768]{0:T(1024)}, u32[]{:S(2)}) copy-start(f32[768]{0:T(1024)} %param.48) | copy-start | bytes 9220
  501.9 72.4 %copy-start.39 = (f32[768]{0:T(1024)S(1)}, f32[768]{0:T(1024)}, u32[]{:S(2)}) copy-start(f32[768]{0:T(1024)} %param.49) | copy-start | bytes 9220
  501.9 117.4 %reduce-scatter.20.cloned.1.call-start = ((), (), s32[]{:S(2)}) async-start(), calls=%async_computation.13 | async-start | bytes 1966080 | tf_op jit(solution)/shard_map/reduce_scatter | solution.py:234
  590.0 55.1 %copy-start.54 = (f32[768]{0:T(1024)S(1)}, f32[768]{0:T(1024)}, u32[]{:S(2)}) copy-start(f32[768]{0:T(1024)} %param.54) | copy-start | bytes 9220
  590.0 55.1 %reduce-scatter.18.cloned.1.call-start = ((), (), s32[]{:S(2)}) async-start(), calls=%async_computation.12 | async-start | bytes 983040 | tf_op jit(solution)/shard_map/reduce_scatter | solution.py:224
  592.6 418.3 %reduce-scatter.34.cloned.1.call-start = ((), (), s32[]{:S(2)}) async-start(), calls=%async_computation.20 | async-start | bytes 884736
  688.2 260.0 %copy-start.13 = (bf16[768,192]{1,0:T(8,128)(2,1)S(1)}, bf16[768,192]{1,0:T(8,128)(2,1)}, u32[]{:S(2)}) copy-start(bf16[768,192]{1,0:T(8,128)(2,1)} %copy-done.12) | copy-start | bytes 884740
  688.2 260.0 %copy-start.28 = (bf16[4,128,8,24]{1,0,3,2:T(4,128)(2,1)S(1)}, bf16[4,128,8,24]{1,0,3,2:T(4,128)(2,1)}, u32[]{:S(2)}) copy-start(bf16[4,128,8,24]{1,0,3,2:T(4,128)(2,1)} %copy.115) | copy-start | bytes 589828
  947.9 92.6 %reduce-scatter.22.cloned.1.call-start = ((), (), s32[]{:S(2)}) async-start(), calls=%async_computation.14 | async-start | bytes 1966080 | tf_op jit(solution)/shard_map/reduce_scatter | solution.py:287
  951.6 155.5 %reduce-scatter.32.cloned.1.call-start = ((), (), s32[]{:S(2)}) async-start(), calls=%async_computation.19 | async-start | bytes 884736 | tf_op jit(solution)/shard_map/reduce_scatter | solution.py:294
  954.0 218.4 %reduce-scatter.36.cloned.1.call-start = ((), (), s32[]{:S(2)}) async-start(), calls=%async_computation.21 | async-start | bytes 884736
  955.6 282.5 %reduce-scatter.30.cloned.1.call-start = ((), (), s32[]{:S(2)}) async-start(), calls=%async_computation.18 | async-start | bytes 884736 | tf_op jit(solution)/shard_map/reduce_scatter | solution.py:293
  957.1 346.3 %reduce-scatter.24.cloned.1.call-start = ((), (), s32[]{:S(2)}) async-start(), calls=%async_computation.15 | async-start | bytes 884736 | tf_op jit(solution)/shard_map/reduce_scatter | solution.py:290
  958.5 410.5 %reduce-scatter.26.cloned.1.call-start = ((), (), s32[]{:S(2)}) async-start(), calls=%async_computation.16 | async-start | bytes 884736 | tf_op jit(solution)/shard_map/reduce_scatter | solution.py:291
  959.8 80.7 %copy-start.4 = (f32[128,768]{1,0:T(8,128)S(1)}, f32[128,768]{1,0:T(8,128)}, u32[]{:S(2)}) copy-start(f32[128,768]{1,0:T(8,128)} %param.34) | copy-start | bytes 1179652
  959.8 80.7 %copy-start.41 = (f32[768]{0:T(1024)S(1)}, f32[768]{0:T(1024)}, u32[]{:S(2)}) copy-start(f32[768]{0:T(1024)} %param.38) | copy-start | bytes 9220
  959.8 80.7 %copy-start.47 = (f32[128]{0:T(128)S(1)}, f32[128]{0:T(128)}, u32[]{:S(2)}) copy-start(f32[128]{0:T(128)} %copy-done.46) | copy-start | bytes 1540
  959.8 80.7 %copy-start.49 = (f32[128]{0:T(128)S(1)}, f32[128]{0:T(128)}, u32[]{:S(2)}) copy-start(f32[128]{0:T(128)} %copy-done.48) | copy-start | bytes 1540
  959.9 81.9 %copy-start.42 = (f32[768]{0:T(1024)S(1)}, f32[768]{0:T(1024)}, u32[]{:S(2)}) copy-start(f32[768]{0:T(1024)} %get-tuple-element.606) | copy-start | bytes 9220
  959.9 81.9 %copy-start.43 = (f32[768]{0:T(1024)S(1)}, f32[768]{0:T(1024)}, u32[]{:S(2)}) copy-start(f32[768]{0:T(1024)} %get-tuple-element.485) | copy-start | bytes 9220
  959.9 81.9 %copy-start.44 = (f32[768]{0:T(1024)S(1)}, f32[768]{0:T(1024)}, u32[]{:S(2)}) copy-start(f32[768]{0:T(1024)} %get-tuple-element.491) | copy-start | bytes 9220
  959.9 81.9 %copy-start.45 = (f32[768]{0:T(1024)S(1)}, f32[768]{0:T(1024)}, u32[]{:S(2)}) copy-start(f32[768]{0:T(1024)} %get-tuple-element.588) | copy-start | bytes 9220
  959.9 125.2 %copy-start.11 = (f32[128,768]{1,0:T(8,128)S(1)}, f32[128,768]{1,0:T(8,128)}, u32[]{:S(2)}) copy-start(f32[128,768]{1,0:T(8,128)} %copy-done.10) | copy-start | bytes 1179652
  959.9 474.4 %reduce-scatter.28.cloned.1.call-start = ((), (), s32[]{:S(2)}) async-start(), calls=%async_computation.17 | async-start | bytes 884736 | tf_op jit(solution)/shard_map/reduce_scatter | solution.py:292
  (40 other events, 441.8 us)
Sparse Core Ops, SparseCore 0:
  502.0 27.9 reduce-scatter.15
  590.2 29.0 reduce-scatter.19
  621.8 23.2 reduce-scatter.17
  948.0 62.8 reduce-scatter.33
  1013.3 27.1 reduce-scatter.21
  1044.6 62.3 reduce-scatter.31
  1110.9 61.4 reduce-scatter.35
  1176.6 61.4 reduce-scatter.29
  1242.0 61.3 reduce-scatter.23
  1307.5 61.4 reduce-scatter.25
  1372.8 61.4 reduce-scatter.27
where the time goes:
time: 1440 us
  matrix products  487 us (34%)
  waiting for transfers between devices  475 us (33%)
  blocking collectives  294 us (20%)
  local copies, waits for them, and re-layouts  77.8 us (5%)
  loops' own time  63.7 us (4%)
  other arithmetic  28.2 us (2%)
  between operations  14.7 us (1%)
    dot_general x42, matrix products, contract_last(): lax.dot_general(left, right, (((1,), (1,)), ((), ())), preferred_element_...  252 us
    dot_general x42, matrix products, contract_first(): lax.dot_general(left, right, (((0,), (0,)), ((), ())), preferred_element_...  219 us
    unnamed x13, waiting for transfers between devices  114 us
    reduce_scatter x1, waiting for transfers between devices, local(): lax.psum_scatter(grad_w_o, 'dp', scatter_dimension=0, tiled=True)  65.7 us
    reduce_scatter x1, waiting for transfers between devices, local(): lax.psum_scatter(grad_w_k, 'dp', scatter_dimension=0, tiled=True)  65.5 us
    reduce_scatter x1, waiting for transfers between devices, local(): lax.psum_scatter(grad_w_v, 'dp', scatter_dimension=0, tiled=True)  65.4 us
    reduce_scatter x1, waiting for transfers between devices, local(): lax.psum_scatter(grad_w_q, 'dp', scatter_dimension=0, tiled=True)  65.3 us
    another operation x4, loops' own time, pair_bias(): lax.map(block_terms, jnp.arange(count // width, dtype=jnp.int32) * width)  62.5 us
  transfers between devices with their start and end apart: 11, of which 10 were waited for; matrix products, arithmetic and copies ran while one was open for 2% of the time, Pallas kernels for 0%

commit v1 on v0

--- a/solution.py
+++ b/solution.py
@@ -6,6 +6,28 @@
 epsilon = 1e-05
 masked_score = -1e30
 pair_block = 2048
+
+
+def joined_along(tiles, dim):
+    tiles = jnp.moveaxis(tiles, 0, dim)
+    lengths = tiles.shape
+    return tiles.reshape(*lengths[:dim], lengths[dim] * lengths[dim + 1], *lengths[dim + 2 :])
+
+
+def collect(x, axis, dim):
+    size = lax.axis_size(axis)
+    pairs = [(i, (i + 1) % size) for i in range(size)]
+    back = [(b, a) for a, b in pairs]
+    lower, upper = ([], [])
+    for step in range(size - 1):
+        if step % 2 == 0:
+            lower.append(lax.ppermute(lower[-1] if lower else x, axis, pairs))
+        else:
+            upper.append(lax.ppermute(upper[-1] if upper else x, axis, back))
+    pieces = jnp.stack([*lower[::-1], x, *upper])
+    shift = lax.axis_index(axis) - len(lower)
+    pieces = pieces[(jnp.arange(size) - shift) % size]
+    return joined_along(pieces, dim)
 
 
 def normalize(values):
@@ -182,7 +204,7 @@
         lax.all_gather(w_o, "dp", axis=0, tiled=True),
         lax.all_gather(w_in, "dp", axis=0, tiled=True),
         lax.all_gather(w_out, "dp", axis=0, tiled=True),
-        lax.all_gather(edge_table, "dp", axis=0, tiled=True),
+        collect(edge_table, "dp", 0),
     )
     full_q, full_k, full_v, full_o, full_in, full_out, full_edge = gathered
     first_normed, first_scale = normalize(layer_in)

time: 1440 us -> 1450 us (level)
  blocking collectives: 294 us -> 267 us
  starting transfers between devices: 0.68 us -> 16.3 us
    all_gather x1 -> x0, blocking collectives: 32.5 us -> none  [local(): lax.all_gather(edge_table, 'dp', axis=0, tiled=True)]
    ppermute x0 -> x7, starting transfers between devices: none -> 15.6 us  [the longest x3 12.6 us: collect(): upper.append(lax.ppermute(upper[-1] if upper else x, axis, back))]
  transfers between devices with their start and end apart: 11 -> 18, of which waited for: 10 -> 13; matrix products, arithmetic and copies ran while one was open for 2% -> 2% of each run, Pallas kernels for 0% -> 0%
where the time goes in v1:
time: 1450 us; the launch traced here: 1440 us
  matrix products  498 us (34%)
  waiting for transfers between devices  483 us (33%)
  blocking collectives  267 us (18%)
  local copies, waits for them, and re-layouts  72.3 us (5%)
  loops' own time  63.7 us (4%)
  other arithmetic  29.4 us (2%)
  starting transfers between devices  16.3 us (1%)
  between operations  14.8 us (1%)
    dot_general x42, matrix products, contract_last(): lax.dot_general(left, right, (((1,), (1,)), ((), ())), preferred_element_...  253 us
    dot_general x42, matrix products, contract_first(): lax.dot_general(left, right, (((0,), (0,)), ((), ())), preferred_element_...  219 us
    unnamed x13, waiting for transfers between devices  114 us
    reduce_scatter x1, waiting for transfers between devices, local(): lax.psum_scatter(grad_w_o, 'dp', scatter_dimension=0, tiled=True)  65.7 us
    reduce_scatter x1, waiting for transfers between devices, local(): lax.psum_scatter(grad_w_k, 'dp', scatter_dimension=0, tiled=True)  65.6 us
    reduce_scatter x1, waiting for transfers between devices, local(): lax.psum_scatter(grad_w_q, 'dp', scatter_dimension=0, tiled=True)  65.3 us
    reduce_scatter x1, waiting for transfers between devices, local(): lax.psum_scatter(grad_w_v, 'dp', scatter_dimension=0, tiled=True)  65.3 us
    another operation x4, loops' own time, pair_bias(): lax.map(block_terms, jnp.arange(count // width, dtype=jnp.int32) * width)  62.5 us
  transfers between devices with their start and end apart: 18, of which 13 were waited for; matrix products, arithmetic and copies ran while one was open for 2% of the time, Pallas kernels for 0%

profile of v1, /device:TPU:0, one launch (start us, length us, event | category | flops | bytes accessed | tf_op | source)
XLA Modules:
  0.0 1443.5 jit_solution(10700955633024108148)
XLA Ops:
  16.9 8.8 all_gather.30
  25.6 31.1 %all_gather.31 = bf16[768,192]{1,0:T(8,128)(2,1)S(1)} all-gather(bf16[96,192]{1,0:T(8,128)(2,1)S(1)} %copy-done.42), channel_id=1, replica_groups=mesh['dp'=8,'mp'=4] {'dp'}, dimensions={0}, use_global_device_ids=true | all-gather | bytes 331776 | tf_op jit(solution)/shard_map/all_gather | solution.py:203
  56.8 31.1 %all_gather.32 = bf16[768,192]{1,0:T(8,128)(2,1)S(1)} all-gather(bf16[96,192]{1,0:T(8,128)(2,1)S(1)} %copy-done.43), channel_id=1, replica_groups=mesh['dp'=8,'mp'=4] {'dp'}, dimensions={0}, use_global_device_ids=true | all-gather | bytes 331776 | tf_op jit(solution)/shard_map/all_gather | solution.py:201
  87.9 31.2 %all_gather.33 = bf16[768,192]{1,0:T(8,128)(2,1)S(1)} all-gather(bf16[96,192]{1,0:T(8,128)(2,1)S(1)} %copy-done.44), channel_id=1, replica_groups=mesh['dp'=8,'mp'=4] {'dp'}, dimensions={0}, use_global_device_ids=true | all-gather | bytes 331776 | tf_op jit(solution)/shard_map/all_gather | solution.py:202
  120.5 33.0 %all_gather.34 = bf16[768,192]{1,0:T(8,128)(2,1)} all-gather(bf16[96,192]{1,0:T(8,128)(2,1)S(1)} %copy-done.45), channel_id=1, replica_groups=mesh['dp'=8,'mp'=4] {'dp'}, dimensions={0}, use_global_device_ids=true | all-gather | bytes 331776 | tf_op jit(solution)/shard_map/all_gather | solution.py:204
  175.8 303.6 %while.76 = (s32[]{:T(128)}, f32[4,8,16384]{2,1,0:T(8,128)}, s32[4,128,128]{2,1,0:T(8,128)}, bf16[22,8]{0,1:T(8,128)(2,1)S(1)}, s32[4,5,128,128]{3,2,1,0:T(8,128...) while((s32[]{:T(128)}, f32[4,8,16384]{2,1,0:T(8,128)}, ...), condition=%wide.region_5.6_spmd, body=%wide.region_2.5_spmd.sunk | while | flops 119668880 | bytes 3820008 | solution.py:226
  176.1 73.4 %while.81 = (s32[]{:T(128)}, f32[8,8,2048]{2,1,0:T(8,128)S(1)}, s32[8]{0:T(128)S(1)}, s32[5,16384]{1,0:T(8,128)S(1)}, bf16[1536,8]{0,1:T(8,128)(2,1)S(1)}, /*ind...) while((s32[]{:T(128)}, f32[8,8,2048]{2,1,0:T(8,128)S(1)}, s32[8]{0:T(128)S(1)}, ...), condition=%wide.region_4.4_spmd, body=%wide.region_3.3_spmd.sunk | while | flops 113246216 | bytes 213227 | solution.py:92
  252.0 73.4 %while.81 = (s32[]{:T(128)}, f32[8,8,2048]{2,1,0:T(8,128)S(1)}, s32[8]{0:T(128)S(1)}, s32[5,16384]{1,0:T(8,128)S(1)}, bf16[1536,8]{0,1:T(8,128)(2,1)S(1)}, /*ind...) while((s32[]{:T(128)}, f32[8,8,2048]{2,1,0:T(8,128)S(1)}, s32[8]{0:T(128)S(1)}, ...), condition=%wide.region_4.4_spmd, body=%wide.region_3.3_spmd.sunk | while | flops 113246216 | bytes 213227 | solution.py:92
  327.9 73.4 %while.81 = (s32[]{:T(128)}, f32[8,8,2048]{2,1,0:T(8,128)S(1)}, s32[8]{0:T(128)S(1)}, s32[5,16384]{1,0:T(8,128)S(1)}, bf16[1536,8]{0,1:T(8,128)(2,1)S(1)}, /*ind...) while((s32[]{:T(128)}, f32[8,8,2048]{2,1,0:T(8,128)S(1)}, s32[8]{0:T(128)S(1)}, ...), condition=%wide.region_4.4_spmd, body=%wide.region_3.3_spmd.sunk | while | flops 113246216 | bytes 213227 | solution.py:92
  403.8 73.4 %while.81 = (s32[]{:T(128)}, f32[8,8,2048]{2,1,0:T(8,128)S(1)}, s32[8]{0:T(128)S(1)}, s32[5,16384]{1,0:T(8,128)S(1)}, bf16[1536,8]{0,1:T(8,128)(2,1)S(1)}, /*ind...) while((s32[]{:T(128)}, f32[8,8,2048]{2,1,0:T(8,128)S(1)}, s32[8]{0:T(128)S(1)}, ...), condition=%wide.region_4.4_spmd, body=%wide.region_3.3_spmd.sunk | while | flops 113246216 | bytes 213227 | solution.py:92
  479.5 16.4 %while.77 = (s32[]{:T(128)}, bf16[4,128,8,24]{1,3,2,0:T(8,128)(2,1)S(1)}, f32[4,8,128,1]{2,1,3,0:T(8,128)S(1)}, bf16[4,128,8,24]{1,3,2,0:T(8,128)(2,1)}, s32[4]{...) while((s32[]{:T(128)}, ...), condition=%wide.region_9.10_spmd, body=%wide.region_6.9_spmd.sunk | while | flops 13786242 | bytes 5475061 | solution.py:232
  497.8 31.5 %all_gather.36 = bf16[768,192]{1,0:T(8,128)(2,1)S(1)} all-gather(bf16[96,192]{1,0:T(8,128)(2,1)S(1)} %copy-done.46), channel_id=1, replica_groups=mesh['dp'=8,'mp'=4] {'dp'}, dimensions={0}, use_global_device_ids=true | all-gather | bytes 331776 | tf_op jit(solution)/shard_map/all_gather | solution.py:205
  529.4 33.0 %all_gather.37 = bf16[768,192]{1,0:T(8,128)(2,1)} all-gather(bf16[96,192]{1,0:T(8,128)(2,1)S(1)} %copy-done.47), channel_id=1, replica_groups=mesh['dp'=8,'mp'=4] {'dp'}, dimensions={0}, use_global_device_ids=true | all-gather | bytes 331776 | tf_op jit(solution)/shard_map/all_gather | solution.py:206
  564.1 9.0 all_gather.38
  574.7 8.7 all_gather.35
  592.0 25.6 %reduce-scatter.20.cloned.1.call-done = f32[128,768]{1,0:T(8,128)} async-done(((f32[512,768]{1,0:T(8,128)}), f32[128,768]{1,0:T(8,128)}) %reduce-scatter.20.cloned.1.call-update) | async-done | bytes 393232 | tf_op jit(solution)/shard_map/reduce_scatter | solution.py:256
  619.4 24.0 %reduce-scatter.18.cloned.1.call-done = bf16[128,768]{1,0:T(8,128)(2,1)} async-done(((bf16[512,768]{1,0:T(8,128)(2,1)}), bf16[128,768]{1,0:T(8,128)(2,1)}) %reduce-scatter.18.cloned.1.call-update) | async-done | bytes 196624 | tf_op jit(solution)/shard_map/reduce_scatter | solution.py:246
  657.8 30.7 %while.78 = (s32[]{:T(128)}, bf16[4,128,8,24]{1,3,2,0:T(8,128)(2,1)}, bf16[4,128,8,24]{1,3,2,0:T(8,128)(2,1)}, bf16[4,128,8,24]{1,3,2,0:T(8,128)(2,1)}, bf16[4,8...) while((s32[]{:T(128)}, ...), condition=%wide.region_19.20_spmd, body=%wide.region_17.19_spmd.sunk | while | flops 32889984 | bytes 9169173 | solution.py:270
  695.0 254.6 %while.80 = (s32[]{:T(128)}, f32[22,8]{0,1:T(8,128)S(1)}, f32[1536,8]{0,1:T(8,128)S(1)}, s32[4,128,128]{2,1,0:T(8,128)}, bf16[4,8,16384]{2,1,0:T(8,128)(2,1)}, /...) while((s32[]{:T(128)}, f32[22,8]{0,1:T(8,128)S(1)}, ...), condition=%wide.region_37.38_spmd.clone, body=%wide.region_34.37_spmd.clone.sunk | while | flops 119419368 | bytes 2550782 | solution.py:293
  697.6 61.1 %while.82 = (s32[]{:T(128)}, f32[1536,8]{0,1:T(8,128)S(1)}, s32[5,16384]{1,0:T(8,128)S(1)}, bf16[8,16384]{1,0:T(8,128)(2,1)S(1)}, s32[]{:T(128)}, /*index=5*/s32...) while((s32[]{:T(128)}, f32[1536,8]{0,1:T(8,128)S(1)}, s32[5,16384]{1,0:T(8,128)S(1)}, ...), condition=%wide.region_36.36_spmd, body=%wide.region_35.35_spmd.sunk | while | flops 113258504 | bytes 254187 | solution.py:162
  761.2 61.1 %while.82 = (s32[]{:T(128)}, f32[1536,8]{0,1:T(8,128)S(1)}, s32[5,16384]{1,0:T(8,128)S(1)}, bf16[8,16384]{1,0:T(8,128)(2,1)S(1)}, s32[]{:T(128)}, /*index=5*/s32...) while((s32[]{:T(128)}, f32[1536,8]{0,1:T(8,128)S(1)}, s32[5,16384]{1,0:T(8,128)S(1)}, ...), condition=%wide.region_36.36_spmd, body=%wide.region_35.35_spmd.sunk | while | flops 113258504 | bytes 254187 | solution.py:162
  824.8 61.1 %while.82 = (s32[]{:T(128)}, f32[1536,8]{0,1:T(8,128)S(1)}, s32[5,16384]{1,0:T(8,128)S(1)}, bf16[8,16384]{1,0:T(8,128)(2,1)S(1)}, s32[]{:T(128)}, /*index=5*/s32...) while((s32[]{:T(128)}, f32[1536,8]{0,1:T(8,128)S(1)}, s32[5,16384]{1,0:T(8,128)S(1)}, ...), condition=%wide.region_36.36_spmd, body=%wide.region_35.35_spmd.sunk | while | flops 113258504 | bytes 254187 | solution.py:162
  888.5 61.1 %while.82 = (s32[]{:T(128)}, f32[1536,8]{0,1:T(8,128)S(1)}, s32[5,16384]{1,0:T(8,128)S(1)}, bf16[8,16384]{1,0:T(8,128)(2,1)S(1)}, s32[]{:T(128)}, /*index=5*/s32...) while((s32[]{:T(128)}, f32[1536,8]{0,1:T(8,128)S(1)}, s32[5,16384]{1,0:T(8,128)S(1)}, ...), condition=%wide.region_36.36_spmd, body=%wide.region_35.35_spmd.sunk | while | flops 113258504 | bytes 254187 | solution.py:162
  965.3 48.5 %reduce-scatter.34.cloned.1.call-done = f32[192,8]{1,0:T(8,128)} async-done(((f32[1536,8]{1,0:T(8,128)}), f32[192,8]{1,0:T(8,128)}) %reduce-scatter.34.cloned.1.call-update) | async-done | bytes 6160
  1015.3 27.9 %reduce-scatter.22.cloned.1.call-done = f32[128,768]{1,0:T(8,128)} async-done(((f32[512,768]{1,0:T(8,128)}), f32[128,768]{1,0:T(8,128)}) %reduce-scatter.22.cloned.1.call-update) | async-done | bytes 393232 | tf_op jit(solution)/shard_map/reduce_scatter | solution.py:309
  1044.6 40.8 %all-reduce = (f32[768]{0:T(1024)}, f32[768]{0:T(1024)}, f32[768]{0:T(1024)S(1)}, f32[768]{0:T(1024)S(1)}, f32[22,32]{0,1:T(8,128)S(1)}, /*index=5*/f32[768]{0:T...) all-reduce(f32[768]{0:T(1024)S(1)} %get-tuple-element.448, ...), channel_id=1, replica_groups=mesh['dp'=8,'mp'=4] {'dp','mp'}, use_global_device_ids=true, to_apply=%region_24.25 | all-reduce | flops 7616 | bytes 60928 | tf_op jit(solution)/shard_map/psum | solution.py:341
  1089.8 20.0 %reduce-scatter.32.cloned.1.call-done = f32[96,192]{1,0:T(8,128)} async-done(((f32[768,192]{1,0:T(8,128)}), f32[96,192]{1,0:T(8,128)}) %reduce-scatter.32.cloned.1.call-update) | async-done | bytes 73744 | tf_op jit(solution)/shard_map/reduce_scatter | solution.py:316
  1109.9 65.3 %reduce-scatter.36.cloned.1.call-done = f32[96,192]{1,0:T(8,128)} async-done(((f32[768,192]{1,0:T(8,128)}), f32[96,192]{1,0:T(8,128)}) %reduce-scatter.36.cloned.1.call-update) | async-done | bytes 73744
  1175.2 65.7 %reduce-scatter.30.cloned.1.call-done = f32[96,192]{1,0:T(8,128)} async-done(((f32[768,192]{1,0:T(8,128)}), f32[96,192]{1,0:T(8,128)}) %reduce-scatter.30.cloned.1.call-update) | async-done | bytes 73744 | tf_op jit(solution)/shard_map/reduce_scatter | solution.py:315
  1240.8 65.3 %reduce-scatter.24.cloned.1.call-done = f32[96,192]{1,0:T(8,128)} async-done(((f32[768,192]{1,0:T(8,128)}), f32[96,192]{1,0:T(8,128)}) %reduce-scatter.24.cloned.1.call-update) | async-done | bytes 73744 | tf_op jit(solution)/shard_map/reduce_scatter | solution.py:312
  1306.2 65.6 %reduce-scatter.26.cloned.1.call-done = f32[96,192]{1,0:T(8,128)} async-done(((f32[768,192]{1,0:T(8,128)}), f32[96,192]{1,0:T(8,128)}) %reduce-scatter.26.cloned.1.call-update) | async-done | bytes 73744 | tf_op jit(solution)/shard_map/reduce_scatter | solution.py:313
  1371.7 65.3 %reduce-scatter.28.cloned.1.call-done = f32[96,192]{1,0:T(8,128)} async-done(((f32[768,192]{1,0:T(8,128)}), f32[96,192]{1,0:T(8,128)}) %reduce-scatter.28.cloned.1.call-update) | async-done | bytes 73744 | tf_op jit(solution)/shard_map/reduce_scatter | solution.py:314
  (577 shorter events, 633.7 us)
Async XLA Ops:
  7.2 146.3 %copy-start = (bf16[22,32]{1,0:T(8,128)(2,1)S(1)}, bf16[22,32]{1,0:T(8,128)(2,1)}, u32[]{:S(2)}) copy-start(bf16[22,32]{1,0:T(8,128)(2,1)} %param.45) | copy-start | bytes 4228
  7.2 565.8 %reduce-scatter.16.cloned.1.call-start = ((), (), s32[]{:S(2)}) async-start(), calls=%async_computation.11 | async-start | bytes 1966080 | tf_op jit(solution)/shard_map/reduce_scatter | solution.py:236
  7.3 146.2 %collective-permute-start = (bf16[192,32]{0,1:T(8,128)(2,1)}, bf16[192,32]{0,1:T(8,128)(2,1)S(1)}, u32[]{:S(2)}, u32[]{:S(2)}) collective-permute-start(bf16[192,32]{0,1:T(8,128)(2,1)} %param.46), channel_id=1, source_target_pairs={{0,4},{4,8},{8,12},{12,16},{16,20},{20,24},{24,28},{28,0},{1,5},{5... | collective-permute-start | bytes 36872 | tf_op jit(solution)/shard_map/ppermute | solution.py:24
  10.3 149.7 %collective-permute-start.4 = (bf16[192,32]{0,1:T(8,128)(2,1)}, bf16[192,32]{0,1:T(8,128)(2,1)S(1)}, u32[]{:S(2)}, u32[]{:S(2)}) collective-permute-start(bf16[192,32]{0,1:T(8,128)(2,1)} %param.46), channel_id=1, source_target_pairs={{4,0},{8,4},{12,8},{16,12},{20,16},{24,20},{28,24},{0,28},{5,1},{9... | collective-permute-start | bytes 36872 | tf_op jit(solution)/shard_map/ppermute | solution.py:26
  14.5 105.0 %copy-start.56 = (f32[128]{0:T(128)}, f32[128]{0:T(128)S(1)}, u32[]{:S(2)}) copy-start(f32[128]{0:T(128)S(1)} %broadcast_multiply_fusion.7) | copy-start | bytes 1540
  15.7 103.9 %copy-start.58 = (f32[128]{0:T(128)}, f32[128]{0:T(128)S(1)}, u32[]{:S(2)}) copy-start(f32[128]{0:T(128)S(1)} %add_rsqrt_fusion.1) | copy-start | bytes 1540
  15.7 103.9 %copy-start.63 = (f32[192]{0:T(256)S(1)}, f32[192]{0:T(256)}, u32[]{:S(2)}) copy-start(f32[192]{0:T(256)} %param.44) | copy-start | bytes 2308
  25.6 94.8 %copy-start.1 = (bf16[512,768]{1,0:T(8,128)(2,1)}, bf16[512,768]{1,0:T(8,128)(2,1)S(1)}, u32[]{:S(2)}) copy-start(bf16[512,768]{1,0:T(8,128)(2,1)S(1)} %all_gather.30) | copy-start | bytes 2359300
  25.6 94.4 %copy-start.64 = (f32[192]{0:T(256)S(1)}, f32[192]{0:T(256)}, u32[]{:S(2)}) copy-start(f32[192]{0:T(256)} %param.43) | copy-start | bytes 2308
  153.5 6.5 collective-permute-start.1
  159.9 6.4 collective-permute-start.2
  160.0 8.8 collective-permute-start.5
  166.4 7.1 collective-permute-start.3
  168.8 6.1 collective-permute-start.6
  175.8 303.7 %copy-start.11 = (bf16[4,128,8,24]{1,3,2,0:T(8,128)(2,1)S(1)}, bf16[4,128,8,24]{1,3,2,0:T(8,128)(2,1)}, u32[]{:S(2)}) copy-start(bf16[4,128,8,24]{1,3,2,0:T(8,128)(2,1)} %copy.86) | copy-start | bytes 589828
  175.8 303.7 %copy-start.12 = (bf16[4,128,8,24]{1,3,2,0:T(8,128)(2,1)S(1)}, bf16[4,128,8,24]{1,3,2,0:T(8,128)(2,1)}, u32[]{:S(2)}) copy-start(bf16[4,128,8,24]{1,3,2,0:T(8,128)(2,1)} %copy.87) | copy-start | bytes 589828
  175.8 303.7 %copy-start.50 = (f32[4,8,128,1]{2,1,3,0:T(8,128)S(1)}, f32[4,8,128,1]{2,1,3,0:T(8,128)}, u32[]{:S(2)}) copy-start(f32[4,8,128,1]{2,1,3,0:T(8,128)} %custom-call.6) | copy-start | bytes 49156
  175.8 303.7 %copy-start.67 = (s32[4]{0:T(128)S(1)}, s32[4]{0:T(128)}, u32[]{:S(2)}) copy-start(s32[4]{0:T(128)} %param.35) | copy-start | bytes 52
  497.8 119.8 %reduce-scatter.20.cloned.1.call-start = ((), (), s32[]{:S(2)}) async-start(), calls=%async_computation.13 | async-start | bytes 1966080 | tf_op jit(solution)/shard_map/reduce_scatter | solution.py:256
  588.7 54.7 %reduce-scatter.18.cloned.1.call-start = ((), (), s32[]{:S(2)}) async-start(), calls=%async_computation.12 | async-start | bytes 983040 | tf_op jit(solution)/shard_map/reduce_scatter | solution.py:246
  592.0 421.8 %reduce-scatter.34.cloned.1.call-start = ((), (), s32[]{:S(2)}) async-start(), calls=%async_computation.20 | async-start | bytes 884736
  694.9 256.1 %copy-start.20 = (bf16[768,192]{1,0:T(8,128)(2,1)S(1)}, bf16[768,192]{1,0:T(8,128)(2,1)}, u32[]{:S(2)}) copy-start(bf16[768,192]{1,0:T(8,128)(2,1)} %copy-done.19) | copy-start | bytes 884740
  694.9 256.1 %copy-start.35 = (bf16[4,128,8,24]{1,0,3,2:T(4,128)(2,1)S(1)}, bf16[4,128,8,24]{1,0,3,2:T(4,128)(2,1)}, u32[]{:S(2)}) copy-start(bf16[4,128,8,24]{1,0,3,2:T(4,128)(2,1)} %copy.95) | copy-start | bytes 589828
  950.8 92.5 %reduce-scatter.22.cloned.1.call-start = ((), (), s32[]{:S(2)}) async-start(), calls=%async_computation.14 | async-start | bytes 1966080 | tf_op jit(solution)/shard_map/reduce_scatter | solution.py:309
  954.4 155.5 %reduce-scatter.32.cloned.1.call-start = ((), (), s32[]{:S(2)}) async-start(), calls=%async_computation.19 | async-start | bytes 884736 | tf_op jit(solution)/shard_map/reduce_scatter | solution.py:316
  956.8 218.3 %reduce-scatter.36.cloned.1.call-start = ((), (), s32[]{:S(2)}) async-start(), calls=%async_computation.21 | async-start | bytes 884736
  958.4 282.4 %reduce-scatter.30.cloned.1.call-start = ((), (), s32[]{:S(2)}) async-start(), calls=%async_computation.18 | async-start | bytes 884736 | tf_op jit(solution)/shard_map/reduce_scatter | solution.py:315
  959.9 346.3 %reduce-scatter.24.cloned.1.call-start = ((), (), s32[]{:S(2)}) async-start(), calls=%async_computation.15 | async-start | bytes 884736 | tf_op jit(solution)/shard_map/reduce_scatter | solution.py:312
  961.3 410.4 %reduce-scatter.26.cloned.1.call-start = ((), (), s32[]{:S(2)}) async-start(), calls=%async_computation.16 | async-start | bytes 884736 | tf_op jit(solution)/shard_map/reduce_scatter | solution.py:313
  962.7 81.8 %copy-start.51 = (f32[768]{0:T(1024)S(1)}, f32[768]{0:T(1024)}, u32[]{:S(2)}) copy-start(f32[768]{0:T(1024)} %get-tuple-element.567) | copy-start | bytes 9220
  962.8 125.1 %copy-start.14 = (f32[128,768]{1,0:T(8,128)S(1)}, f32[128,768]{1,0:T(8,128)}, u32[]{:S(2)}) copy-start(f32[128,768]{1,0:T(8,128)} %copy-done.13) | copy-start | bytes 1179652
  962.8 474.2 %reduce-scatter.28.cloned.1.call-start = ((), (), s32[]{:S(2)}) async-start(), calls=%async_computation.17 | async-start | bytes 884736 | tf_op jit(solution)/shard_map/reduce_scatter | solution.py:314
  (54 other events, 1556.8 us)
Sparse Core Ops, SparseCore 0:
  497.9 29.4 reduce-scatter.15
  588.8 28.7 reduce-scatter.19
  620.1 23.2 reduce-scatter.17
  950.9 62.8 reduce-scatter.33
  1016.1 27.0 reduce-scatter.21
  1047.4 62.4 reduce-scatter.31
  1113.7 61.3 reduce-scatter.35
  1179.4 61.3 reduce-scatter.29
  1244.7 61.4 reduce-scatter.23
  1310.2 61.4 reduce-scatter.25
  1375.6 61.3 reduce-scatter.27
